TPU v7x, 32 devices: a whole 2x2x4 slice. The times are simulated.
32 devices in a mesh: lat: 16 (over z, y, core), lev: 2 (over x).
Axes of the slice: x: 2, y: 2, z: 4, core: 2. Of those that a mesh axis runs over, the one named last changes fastest.
Arguments:
- spectral_in: bfloat16 [2, 336, 2, 1280], P('lev', 'lat'), may hold values from -0.25 to 0.25
- legendre: bfloat16 [2, 336, 640, 32], P('lev', 'lat'), may hold values from -0.25 to 0.25
- slot_wave: int32 [2, 336], replicated, may hold values from 0 to 640, as said below
- row_length: int32 [32], P('lat'), may hold values from 16 to 2688, as said below
- quad_weight: float32 [32], replicated, may hold values from 8 to 64
Outputs:
- grid_field: bfloat16 [2, 32, 2688], P('lev', 'lat')
- spectral_out: bfloat16 [2, 336, 2, 1280], P('lev', 'lat')
Inputs may be any that keep to these rules, and one draw needn't show every extreme that they name: `slot_wave`: each wavenumber 0 to 639 stands in exactly one slot; all other slots hold 640. Each device holds at most 21 of the wavenumbers. `row_length`: lengths are multiples of 4; the two middle rows have length 2688.
All inputs are finite; a program needn't handle non-finite values.
Results may differ from a plain program's by a relative error of at most 0.0072.
Values may be sent and summed in bfloat16 or wider, within the bound.
A program may use at most 64 MiB of HBM per device.

v0:
```python
import math

import jax
import jax.numpy as jnp
from jax import lax
from jax.sharding import PartitionSpec as P

M = 640
NLON = 2688


def transform_row(coeffs_row, length, wave_ids):
    lon_index = jnp.arange(NLON, dtype=jnp.int32)
    phase_turn = wave_ids[:, None] * lon_index[None, :] % length
    step_angle = 2.0 * math.pi / length.astype(jnp.float32)
    angles = phase_turn.astype(jnp.float32) * step_angle
    inside = (lon_index[None, :] < length) & (wave_ids[:, None] < M)
    dft_table = jnp.concatenate(
        [jnp.where(inside, jnp.cos(angles), 0.0), jnp.where(inside, jnp.sin(angles), 0.0)], 0
    ).astype(jnp.bfloat16)
    factor = jnp.where(wave_ids == 0, 1.0, 2.0).astype(jnp.bfloat16)
    stacked = jnp.concatenate(
        [coeffs_row[:, :, 0] * factor[:, None], -(coeffs_row[:, :, 1] * factor[:, None])], 0
    )
    grid_raw = jnp.dot(stacked.T, dft_table, preferred_element_type=jnp.float32)
    shaped = (grid_raw * (1.0 + 0.5 * jnp.tanh(grid_raw))).astype(jnp.bfloat16)
    summed = jnp.dot(shaped, dft_table.T, preferred_element_type=jnp.float32)
    slot_count = wave_ids.shape[0]
    length_float = length.astype(jnp.float32)
    real_back = summed[:, :slot_count] / length_float
    imag_back = -summed[:, slot_count:] / length_float
    four_row = jnp.stack([real_back, imag_back], -1).astype(jnp.bfloat16)
    return (shaped, jnp.transpose(four_row, (1, 0, 2)))


def transpose_lat(blocks):
    lat_index = lax.axis_index("lat")
    return lax.dynamic_index_in_dim(
        lax.all_gather(blocks[None], "lat", axis=0, tiled=True), lat_index, 1, keepdims=False
    )


def shards(spectral_in, legendre, slot_wave, row_length, quad_weight):
    lat_count = lax.axis_size("lat")
    lat_index = lax.axis_index("lat")
    lev_index = lax.axis_index("lev")
    own_lat = spectral_in.shape[1]
    fields = spectral_in.shape[2]
    degrees = legendre.shape[2]
    lat_total = legendre.shape[3]
    lat_local = row_length.shape[0]
    all_waves = slot_wave.reshape(-1)
    my_waves = lax.dynamic_slice(slot_wave, (lev_index, lat_index * own_lat), (1, own_lat)).reshape(
        own_lat
    )
    keep_mask = (jnp.arange(degrees, dtype=jnp.int32)[None, :] >= my_waves[:, None]).astype(
        jnp.bfloat16
    )
    coeffs = spectral_in.reshape(own_lat, fields, 2, degrees) * keep_mask[:, None, None, :]
    coeffs = coeffs.reshape(own_lat, fields * 2, degrees)
    matrices = legendre.reshape(own_lat, degrees, lat_total)
    fourier = jnp.einsum(
        "sqn,snl->lsq", coeffs, matrices, preferred_element_type=jnp.float32
    ).astype(jnp.bfloat16)
    blocks = fourier.reshape(lat_count, lat_local * own_lat * fields * 2)
    arrived = transpose_lat(blocks)
    row_major = jnp.transpose(
        arrived.reshape(lat_count, lat_local, own_lat, fields, 2), (1, 0, 2, 3, 4)
    )
    row_major = row_major.reshape(lat_local, lat_count * own_lat, fields, 2)
    spread = lax.all_to_all(row_major, "lev", split_axis=2, concat_axis=1, tiled=True)

    def one_row(packed):
        return transform_row(packed[0], packed[1], all_waves)

    shaped_rows, four_rows = lax.map(one_row, (spread, row_length))
    grid_field = jnp.transpose(shaped_rows, (1, 0, 2))
    regrouped = lax.all_to_all(four_rows, "lev", split_axis=1, concat_axis=2, tiled=True)
    outgoing = jnp.transpose(
        regrouped.reshape(lat_local, lat_count, own_lat * fields * 2), (1, 0, 2)
    )
    outgoing = outgoing.reshape(lat_count, lat_local * own_lat * fields * 2)
    returned = transpose_lat(outgoing)
    columns = returned.reshape(lat_total, own_lat, fields * 2)
    weighted = (columns * quad_weight[:, None, None]).astype(jnp.bfloat16)
    result = jnp.einsum("lsq,snl->sqn", weighted, matrices, preferred_element_type=jnp.float32)
    result = result * keep_mask[:, None, :].astype(jnp.float32)
    spectral_out = result.reshape(1, own_lat, fields, 2 * degrees).astype(jnp.bfloat16)
    return (grid_field, spectral_out)


def solution(mesh):
    in_specs = (P("lev", "lat", None, None), P("lev", "lat", None, None), P(), P("lat"), P())
    out_specs = (P("lev", "lat", None), P("lev", "lat", None, None))
    return jax.shard_map(shards, mesh=mesh, in_specs=in_specs, out_specs=out_specs, check_vma=False)
```

profile of v0, /device:TPU:0, one launch (start us, length us, event | category | flops | bytes accessed | tf_op | source)
XLA Modules:
  0.0 274.8 jit_solution(8113161795483533223)
XLA Ops:
  0.7 0.8 dynamic-slice_bitcast_fusion.1
  1.6 1.1 reshape.209
  2.7 0.4 fusion.23
  3.1 0.3 copy.58
  3.5 23.4 %all_gather.6 = bf16[16,16,168]{2,1,0:T(8,128)(2,1)S(1)} all-gather(bf16[1,16,168]{2,1,0:T(8,128)(2,1)S(1)} %broadcast_in_dim_reshape.11), channel_id=1, replica_groups=mesh['lat'=16,'lev'=2] {'lat'}, dimensions={0}, use_global_device_ids=true | all-gather | bytes 91392 | tf_op jit(solution)/shard_map/all_gather | solution.py:39
  27.3 0.7 reshape.222
  28.0 3.2 %all-to-all-start = ((bf16[2,336,2,2]{1,3,0,2:T(2,128)(2,1)}), bf16[2,336,2,2]{1,3,0,2:T(2,128)(2,1)S(1)}, u32[]{:S(2)}, u32[]{:S(2)}) async-start(bf16[2,336,2,2]{1,3,0,2:T(2,128)(2,1)} %reshape.222), calls=%async_computation | async-start | bytes 12288 | tf_op jit(solution)/shard_map/all_to_all | solution.py:71
  31.2 0.8 reshape.213
  32.0 3.0 %all-to-all-done = bf16[2,336,2,2]{1,3,0,2:T(2,128)(2,1)S(1)} async-done(((bf16[2,336,2,2]{1,3,0,2:T(2,128)(2,1)}), bf16[2,336,2,2]{1,3,0,2:T(2,128)(2,1)S(1)}, u32[]{:S(2)}, u32[]{:S(2)}) %all-to-all-start) | async-done | bytes 5408 | tf_op jit(solution)/shard_map/all_to_all | solution.py:71
  35.1 212.9 %while.12 = (s32[]{:T(128)}, bf16[2,1,2688]{2,0,1:T(2,128)(2,1)S(1)}, bf16[2,672,1,2]{1,3,2,0:T(2,128)(2,1)S(1)}, bf16[2,672,1,2]{1,3,2,0:T(2,128)(2,1)S(1)}, s3...) while((s32[]{:T(128)}, ...), condition=%wide.region_1.2_spmd, body=%wide.region_0.1_spmd.sunk | while | flops 70482728 | bytes 21799680 | solution.py:76
  35.1 1.2 dynamic_slice.28
  38.3 0.7 iota_compare_fusion.3
  39.0 0.8 broadcast_in_dim_reshape.14
  39.8 98.1 %fusion.40 = (bf16[672,2688]{1,0:T(8,128)(2,1)S(1)}, bf16[672,2688]{1,0:T(8,128)(2,1)S(1)}) fusion(f32[]{:T(128)S(6)} %div.30, s32[]{:T(128)S(6)} %select_n.69, s32[672]{0:T(1024)S(1)} %broadcast_in_dim_reshape.14, pred[]{:T(512)S(6)} %lt.66, pred[2688]{0:T(1024)(128)(4,1)S(1)} %iota_compare_fusion.3, pred[672]{0:T(1024)(128)(4,1)S(1)} %broadcast_compare_fusion.2), kind=kLoop, calls=%fused_computation.3.clone.1 | loop fusion | flops 27095040 | bytes 7231401 | tf_op jit(solution)/shard_map/convert.4
  137.9 1.1 fusion.41
  139.0 2.3 fusion.42
  141.5 1.2 dynamic_slice.28
  144.8 0.7 iota_compare_fusion.3
  145.4 0.8 broadcast_in_dim_reshape.14
  146.2 98.1 %fusion.40 = (bf16[672,2688]{1,0:T(8,128)(2,1)S(1)}, bf16[672,2688]{1,0:T(8,128)(2,1)S(1)}) fusion(f32[]{:T(128)S(6)} %div.30, s32[]{:T(128)S(6)} %select_n.69, s32[672]{0:T(1024)S(1)} %broadcast_in_dim_reshape.14, pred[]{:T(512)S(6)} %lt.66, pred[2688]{0:T(1024)(128)(4,1)S(1)} %iota_compare_fusion.3, pred[672]{0:T(1024)(128)(4,1)S(1)} %broadcast_compare_fusion.2), kind=kLoop, calls=%fused_computation.3.clone.1 | loop fusion | flops 27095040 | bytes 7231401 | tf_op jit(solution)/shard_map/convert.4
  244.4 1.1 fusion.41
  245.5 2.3 fusion.42
  248.0 0.2 copy.64
  248.2 0.3 reshape.225
  248.6 6.1 %all_to_all.33 = bf16[2,2,672]{2,1,0:T(2,128)(2,1)S(1)} all-to-all(bf16[2,2,672]{2,1,0:T(2,128)(2,1)S(1)} %reshape.225), channel_id=1, replica_groups=mesh['lat'=16,'lev'=2] {'lev'}, dimensions={0} | all-to-all | bytes 10752 | tf_op jit(solution)/shard_map/all_to_all | solution.py:78
  254.7 0.4 reshape.226
  255.1 0.2 copy.70
  255.3 0.3 copy.66
  255.8 17.5 %all_gather.7 = bf16[16,16,168]{2,1,0:T(8,128)(2,1)S(1)} all-gather(bf16[1,16,168]{2,1,0:T(8,128)(2,1)S(1)} %broadcast_in_dim_reshape.12), channel_id=1, replica_groups=mesh['lat'=16,'lev'=2] {'lat'}, dimensions={0}, use_global_device_ids=true | all-gather | bytes 91392 | tf_op jit(solution)/shard_map/all_gather | solution.py:39
  273.5 0.2 copy.68
  273.7 0.3 fusion.22
  274.0 0.8 convert_element_type.95
  (40 shorter events, 1.7 us)
Async XLA Ops:
  0.6 2.0 copy-start
  28.0 7.0 %all-to-all-start = ((bf16[2,336,2,2]{1,3,0,2:T(2,128)(2,1)}), bf16[2,336,2,2]{1,3,0,2:T(2,128)(2,1)S(1)}, u32[]{:S(2)}, u32[]{:S(2)}) async-start(bf16[2,336,2,2]{1,3,0,2:T(2,128)(2,1)} %reshape.222), calls=%async_computation | async-start | bytes 12288 | tf_op jit(solution)/shard_map/all_to_all | solution.py:71
  35.1 238.6 %copy-start.1 = (f32[32]{0:T(128)S(1)}, f32[32]{0:T(128)}, u32[]{:S(2)}) copy-start(f32[32]{0:T(128)} %param.11) | copy-start | bytes 388
  248.0 26.8 %copy-start.2 = (bf16[2,1,2688]{2,0,1:T(2,128)(2,1)}, bf16[2,1,2688]{2,0,1:T(2,128)(2,1)S(1)}, u32[]{:S(2)}) copy-start(bf16[2,1,2688]{2,0,1:T(2,128)(2,1)S(1)} %get-tuple-element.40) | copy-start | bytes 32260
where the time goes:
time: 275 us
  other arithmetic  198 us (72%)
  blocking collectives  47 us (17%)
  local copies, waits for them, and re-layouts  11.4 us (4%)
  matrix products  7.28 us (3%)
  loops' own time  4.14 us (2%)
  starting transfers between devices  3.22 us (1%)
  waiting for transfers between devices  3.01 us (1%)
    another operation x2, other arithmetic  196 us
    all_gather x2, blocking collectives, transpose_lat(): lax.all_gather(blocks[None], 'lat', axis=0, tiled=True)  40.9 us
    all_to_all x1, blocking collectives, shards(): lax.all_to_all(four_rows, 'lev', split_axis=1, concat_axis=2, tiled=True)  6.13 us
  transfers between devices with their start and end apart: 1, of which 1 were waited for; matrix products, arithmetic and copies ran while one was open for 0% of the time, Pallas kernels for 0%

commit v1 on v0

v1 whole, which is shorter than its diff:
```python
import functools

import jax
import jax.numpy as jnp
from jax import lax
from jax.experimental import pallas as pl
from jax.experimental.pallas import tpu as pltpu
from jax.sharding import PartitionSpec as P

M = 640
NLON = 2688
LOW = 32
HIGH = 24
STEP = 384
GROUP = 8
F32 = jnp.float32
BF16 = jnp.bfloat16

SIN = (3.1415927410125732, -5.167709827423096, 2.550076961517334, -0.5982866883277893, 0.07764717191457748)
COS = (1.0, -4.934802055358887, 4.058709144592285, -1.3352116346359253, 0.234935462474823, -0.024393025785684586)


def horner(coefs, x):
    total = jnp.full_like(x, coefs[-1])
    for c in coefs[-2::-1]:
        total = total * x + c
    return total


def turn_cos_sin(product, length):
    inverse = 1.0 / length
    rest = product - jnp.round(product * inverse) * length
    t = rest * inverse
    square = t * t
    half_sin = t * horner(SIN, square)
    half_cos = horner(COS, square)
    return 1.0 - 2.0 * half_sin * half_sin, 2.0 * half_sin * half_cos


def dot_nn(a, b):
    return lax.dot_general(a, b, (((1,), (0,)), ((), ())), preferred_element_type=F32)


def dot_nt(a, b):
    return lax.dot_general(a, b, (((1,), (1,)), ((), ())), preferred_element_type=F32)


def split(x):
    high = x.astype(BF16)
    return high, (x - high.astype(F32)).astype(BF16)


def kernel(
    n_lat, n_lev, wave_ref, length_ref, quad_ref, spec_ref, leg_ref, grid_ref, out_ref,
    four, stacked, send1, recv1, send2, recv2, columns, flipped, table_p, table_q, table_b, sems,
):
    n = n_lat * n_lev
    lat = lax.axis_index("lat")
    lev = lax.axis_index("lev")
    me = lev * n_lat + lat
    own, fields = spec_ref.shape[0], spec_ref.shape[1]
    rows, deg = leg_ref.shape[1], leg_ref.shape[2]
    local = length_ref.shape[0]
    per_slot = 2 * fields

    def partner(t):
        other = lax.rem(me + t, n)
        return other, (lax.rem(other, n_lat), lax.div(other, n_lat))

    barrier = pltpu.get_barrier_semaphore()

    def greet(t, carry):
        pl.semaphore_signal(barrier, inc=1, device_id=partner(t)[1], device_id_type=pl.DeviceIdType.MESH)
        return carry

    lax.fori_loop(1, n, greet, 0)

    degree = lax.broadcasted_iota(jnp.int32, (per_slot, deg), 1)
    lane = lax.broadcasted_iota(jnp.int32, (1, 128), 1)
    wave_row = jnp.full((1, 128), float(M), F32)
    four[...] = jnp.zeros_like(four)
    for s in range(own):
        m = wave_ref[lev, lat * own + s]
        x = spec_ref[s].astype(F32)
        x = jnp.concatenate([x[:, :deg], x[:, deg:]], 0)
        x = jnp.where(degree >= m, x, 0.0).astype(BF16)
        four[pl.ds(s * per_slot, per_slot), pl.ds(0, rows)] = dot_nt(x, leg_ref[s]).astype(BF16).astype(F32)
        wave_row = jnp.where(lane // per_slot == s, m.astype(F32), wave_row)
    turned = four[...].T
    for j in range(n_lat):
        send1[j, pl.ds(0, local), :] = turned[j * local : (j + 1) * local, :]
        send1[j, pl.ds(local, 1), :] = wave_row
        send1[j, pl.ds(local + 1, send1.shape[1] - local - 1), :] = jnp.zeros(
            (send1.shape[1] - local - 1, 128), F32
        )

    pl.semaphore_wait(barrier, n - 1)

    def remote(src, dst, k, device):
        return pltpu.make_async_remote_copy(
            src_ref=src, dst_ref=dst, send_sem=sems.at[2 * k], recv_sem=sems.at[2 * k + 1],
            device_id=device, device_id_type=pl.DeviceIdType.MESH,
        )

    def send_rows(t, carry):
        _, device = partner(t)
        remote(send1.at[device[0]], recv1.at[me], 0, device).start()
        return carry

    lax.fori_loop(1, n, send_rows, 0)
    recv1[me] = send1[lat]

    for r in range(local):
        length = jnp.full((1, STEP), length_ref[r].astype(F32), F32)

        def tables(i, carry):
            at = pl.multiple_of(i * STEP, 128)
            k = (lax.broadcasted_iota(jnp.int32, (1, STEP), 1) + at).astype(F32)
            a = lax.broadcasted_iota(jnp.int32, (HIGH, STEP), 0).astype(F32) * float(LOW)
            cos_a, sin_a = turn_cos_sin(a * k, length)
            p = jnp.concatenate([cos_a, -sin_a], 0)
            q = jnp.concatenate([sin_a, cos_a], 0)
            table_p[r, :, pl.ds(at, STEP)] = jnp.concatenate(split(p), 0)
            table_q[r, :, pl.ds(at, STEP)] = jnp.concatenate(split(q), 0)
            b = lax.broadcasted_iota(jnp.int32, (LOW, STEP), 0).astype(F32)
            cos_b, sin_b = turn_cos_sin(b * k, length)
            table_b[r, :, pl.ds(at, STEP)] = jnp.concatenate([cos_b, sin_b], 0)
            return carry

        lax.fori_loop(0, NLON // STEP, tables, 0)

    def all_arrived(buffer, k):
        part = buffer.at[pl.ds(0, n - 1)]
        pltpu.make_async_copy(part, part, sems.at[k]).wait()

    all_arrived(recv1, 1)

    index_a = lax.broadcasted_iota(jnp.int32, (HIGH, 128), 0)
    index_b = lax.broadcasted_iota(jnp.int32, (LOW, 128), 0)
    is_real = lax.rem(lane, per_slot) == lev
    is_imag = lax.rem(lane, per_slot) == lev + fields

    def one_hots(o):
        w = recv1[o, pl.ds(local, 1), :].astype(jnp.int32)
        return index_a == w // LOW, (index_b == w % LOW).astype(F32)

    def place(g, totals):
        lefts = []
        rights = [[] for _ in range(local)]
        for i in range(GROUP):
            o = g * GROUP + i
            hot_a, hot_b = one_hots(o)
            lefts.append(hot_b)
            for r in range(local):
                z = recv1[o, pl.ds(r, 1), :]
                pieces = [
                    jnp.where(hot_a, jnp.where(which, z, 0.0), 0.0) for which in (is_real, is_imag)
                ]
                rights[r].append(jnp.concatenate(pieces, 0))
        left = jnp.concatenate(lefts, 1).astype(BF16)
        return tuple(
            totals[r] + dot_nt(left, jnp.concatenate(rights[r], 1).astype(BF16)) for r in range(local)
        )

    placed = lax.fori_loop(
        0, n // GROUP, place, tuple(jnp.zeros((LOW, 2 * HIGH), F32) for _ in range(local))
    )

    row_b = lax.broadcasted_iota(jnp.int32, (LOW, 2 * HIGH), 0)
    col_a = lax.rem(lax.broadcasted_iota(jnp.int32, (LOW, 2 * HIGH), 1), HIGH)
    factor = jnp.where((row_b == 0) & (col_a == 0), 1.0, 2.0)
    spectra = []
    for r in range(local):
        z = placed[r] * factor
        z = jnp.concatenate([z, z], 1).astype(BF16)
        length_int = length_ref[r]

        def longitudes(i, total):
            at = pl.multiple_of(i * STEP, 128)
            here = pl.ds(at, STEP)
            cos_b = table_b[r, pl.ds(0, LOW), here]
            sin_b = table_b[r, pl.ds(LOW, LOW), here]
            q = table_q[r, :, here]
            raw = jnp.sum(
                dot_nn(z, table_p[r, :, here]) * cos_b - dot_nn(z, q) * sin_b, axis=0, keepdims=True
            )
            shaped = (raw * (1.0 + 0.5 * jnp.tanh(raw))).astype(BF16).astype(F32)
            k = lax.broadcasted_iota(jnp.int32, (1, STEP), 1) + at
            shaped = jnp.where(k < length_int, shaped, 0.0)
            columns[pl.ds(r, 1), here] = shaped
            g = jnp.concatenate([shaped * cos_b, shaped * sin_b], 0)
            return total + dot_nt(q, jnp.concatenate(split(g), 0))

        total = lax.fori_loop(
            0, NLON // STEP, longitudes, jnp.zeros((4 * HIGH, 4 * LOW), F32)
        )
        both = 2 * HIGH
        total = total[:both, : 2 * LOW] + total[both:, : 2 * LOW] + total[:both, 2 * LOW :]
        ss, sc = total[:HIGH, LOW:], total[:HIGH, :LOW]
        cs, cc = total[HIGH:, LOW:], total[HIGH:, :LOW]
        length = jnp.full((HIGH, LOW), length_int.astype(F32), F32)
        weight = quad_ref[lat * local + r]
        for part in (cc - ss, -(sc + cs)):
            spectra.append((part / length).astype(BF16).astype(F32) * weight)
    grid_ref[...] = columns[pl.ds(0, local), :].astype(BF16)
    spectrum = jnp.concatenate(spectra, 0).astype(BF16)

    def pick(g, carry):
        hots = [one_hots(g * GROUP + i) for i in range(GROUP)]
        right = jnp.concatenate([hot_b for _, hot_b in hots], 1).astype(BF16)
        spread = dot_nn(spectrum, right)
        for i in range(GROUP):
            cut = spread[:, i * 128 : (i + 1) * 128]
            lines = []
            for r in range(local):
                line = jnp.zeros((1, 128), F32)
                for c, which in enumerate((is_real, is_imag)):
                    first = (2 * r + c) * HIGH
                    value = jnp.sum(
                        jnp.where(hots[i][0], cut[first : first + HIGH], 0.0), axis=0, keepdims=True
                    )
                    line = jnp.where(which, value, line)
                lines.append(line)
            send2[g * GROUP + i] = jnp.concatenate(lines, 0)
        return carry

    lax.fori_loop(0, n // GROUP, pick, 0)

    def send_slots(t, carry):
        other, device = partner(t)
        remote(send2.at[other], recv2.at[me], 1, device).start()
        return carry

    lax.fori_loop(1, n, send_slots, 0)
    recv2[me] = send2[me]
    all_arrived(recv2, 3)

    for j in range(n_lat):
        value = recv2[j]
        for g in range(1, n_lev):
            value = value + recv2[g * n_lat + j]
        stacked[pl.ds(j * local, local), :] = value
    flipped[...] = stacked[...].T
    for s in range(own):
        m = wave_ref[lev, lat * own + s]
        w = flipped[pl.ds(s * per_slot, per_slot), :].astype(BF16)
        y = jnp.where(degree >= m, dot_nn(w, leg_ref[s]), 0.0)
        out_ref[s] = jnp.concatenate([y[:fields], y[fields:]], 1).astype(BF16)

    all_arrived(recv1, 0)
    all_arrived(recv2, 2)


def shards(n_lat, n_lev, spectral_in, legendre, slot_wave, row_length, quad_weight):
    _, own, fields, double = spectral_in.shape
    _, _, deg, rows = legendre.shape
    local = row_length.shape[0]
    n = n_lat * n_lev
    assert fields == n_lev and own * fields * 2 <= 128 and n % GROUP == 0 and rows % 8 == 0
    rows_up = -(-rows // 128) * 128
    message = 4 if local < 4 else -(-(local + 1) // 8) * 8
    vmem = pl.BlockSpec(memory_space=pltpu.VMEM)
    smem = pl.BlockSpec(memory_space=pltpu.SMEM)
    grid, out = pl.pallas_call(
        functools.partial(kernel, n_lat, n_lev),
        out_shape=(
            jax.ShapeDtypeStruct((local, NLON), BF16),
            jax.ShapeDtypeStruct((own, fields, double), BF16),
        ),
        in_specs=[smem, smem, smem, vmem, vmem],
        out_specs=(vmem, vmem),
        scratch_shapes=[
            pltpu.VMEM((128, rows_up), F32),
            pltpu.VMEM((rows, 128), F32),
            pltpu.VMEM((n_lat, message, 128), F32),
            pltpu.VMEM((n, message, 128), F32),
            pltpu.VMEM((n, local, 128), F32),
            pltpu.VMEM((n, local, 128), F32),
            pltpu.VMEM((8, NLON), F32),
            pltpu.VMEM((128, rows), F32),
            pltpu.VMEM((local, 4 * HIGH, NLON), BF16),
            pltpu.VMEM((local, 4 * HIGH, NLON), BF16),
            pltpu.VMEM((local, 2 * LOW, NLON), F32),
            pltpu.SemaphoreType.DMA((4,)),
        ],
        compiler_params=pltpu.CompilerParams(
            collective_id=0, has_side_effects=True, vmem_limit_bytes=48 * 1024 * 1024
        ),
    )(
        slot_wave, row_length, quad_weight, spectral_in.reshape(own, fields, double),
        jnp.transpose(legendre.reshape(own, deg, rows), (0, 2, 1)),
    )
    return grid[None], out[None]


def solution(mesh):
    in_specs = (P("lev", "lat", None, None), P("lev", "lat", None, None), P(), P("lat"), P())
    out_specs = (P("lev", "lat", None), P("lev", "lat", None, None))
    body = functools.partial(shards, mesh.shape["lat"], mesh.shape["lev"])
    return jax.shard_map(body, mesh=mesh, in_specs=in_specs, out_specs=out_specs, check_vma=False)
```

time: 275 us -> 29.7 us (0.11)
  other arithmetic: 198 us -> 0 us
  blocking collectives: 47 us -> 0 us
  Pallas kernels: 0 us -> 24.2 us
  matrix products: 7.28 us -> 0 us
  local copies, waits for them, and re-layouts: 11.4 us -> 4.63 us
  loops' own time: 4.14 us -> 0 us
  starting transfers between devices: 3.22 us -> 0 us
  waiting for transfers between devices: 3.01 us -> 0 us
    another operation x4 -> x0, other arithmetic: 196 us -> none
    all_gather x2 -> x0, blocking collectives: 40.9 us -> none  [transpose_lat(): lax.all_gather(blocks[None], 'lat', axis=0, tiled=True)]
    pallas_call x0 -> x1, Pallas kernels: none -> 24.2 us  [shards(): pl.pallas_call(functools.partial(kernel, n_lat, n_lev), out_shape=(jax.Sh...]
    dot_general x6 -> x0, matrix products: 7.28 us -> none  [the longest x2 4.54 us: transform_row(): summed = jnp.dot(shaped, dft_table.T, preferred_element_type=jnp.float32)]
    all_to_all x1 -> x0, blocking collectives: 6.13 us -> none  [shards(): lax.all_to_all(four_rows, 'lev', split_axis=1, concat_axis=2, tiled=True)]
    another operation x1 -> x0, loops' own time: 4.14 us -> none  [shards(): shaped_rows, four_rows = lax.map(one_row, (spread, row_length))]
    unnamed x8 -> x12, local copies, waits for them, and re-layouts: 0.7 us -> 4.63 us
    all_to_all x1 -> x0, starting transfers between devices: 3.22 us -> none  [shards(): lax.all_to_all(row_major, 'lev', split_axis=2, concat_axis=1, tiled=True)]
  transfers between devices with their start and end apart: 1 -> 0, of which waited for: 1 -> 0; matrix products, arithmetic and copies ran while one was open for 0% -> 0% of each run, Pallas kernels for 0% -> 0%
where the time goes in v1:
time: 29.7 us; the launch traced here: 29.5 us
  Pallas kernels  24.2 us (81%)
  local copies, waits for them, and re-layouts  4.63 us (16%)
  between operations  0.66 us (2%)
    pallas_call x1, Pallas kernels, shards(): pl.pallas_call(functools.partial(kernel, n_lat, n_lev), out_shape=(jax.Sh...  24.2 us
    unnamed x12, local copies, waits for them, and re-layouts  4.63 us

profile of v1, /device:TPU:0, one launch (start us, length us, event | category | flops | bytes accessed | tf_op | source)
XLA Modules:
  0.0 29.5 jit_solution(523511253791450529)
XLA Ops:
  0.6 0.0 copy-start.2
  0.6 0.0 copy-start.3
  0.7 0.7 %copy-done.2 = s32[2,336]{1,0:T(2,128)S(1)} copy-done((s32[2,336]{1,0:T(2,128)S(1)}, s32[2,336]{1,0:T(2,128)}, u32[]{:S(2)}) %copy-start.2) | copy-done | bytes 2712
  1.3 0.0 copy-done.3
  1.3 0.0 copy-start
  1.3 1.2 %copy-done = bf16[1,21,640,32]{2,3,1,0:T(8,128)(2,1)S(1)} copy-done((bf16[1,21,640,32]{2,3,1,0:T(8,128)(2,1)S(1)}, bf16[1,21,640,32]{2,3,1,0:T(8,128)(2,1)}, u32[]{:S(2)}) %copy-start) | copy-done | bytes 860184
  2.5 0.0 copy-start.1
  2.5 0.9 %copy-done.1 = bf16[1,21,2,1280]{3,2,1,0:T(2,128)(2,1)S(1)} copy-done((bf16[1,21,2,1280]{3,2,1,0:T(2,128)(2,1)S(1)}, bf16[1,21,2,1280]{3,2,1,0:T(2,128)(2,1)}, u32[]{:S(2)}) %copy-start.1) | copy-done | bytes 107544
  3.4 0.0 copy-start.4
  3.4 0.7 %copy-done.4 = f32[32]{0:T(128)S(1)} copy-done((f32[32]{0:T(128)S(1)}, f32[32]{0:T(128)}, u32[]{:S(2)}) %copy-start.4) | copy-done | bytes 152
  4.0 24.2 %shard_map.68 = (bf16[2,2688]{1,0:T(2,128)(2,1)S(1)}, bf16[21,2,1280]{2,1,0:T(2,128)(2,1)S(1)}) custom-call(s32[2,336]{1,0:T(2,128)S(1)} %copy-done.2, s32[2]{0:T(128)S(1)} %copy-done.3, f32[32]{0:T(128)S(1)} %copy-done.4, bf16[21,2,1280]{2,1,0:T(2,128)(2,1)S(1)} %bitcast.7, bf16[21,32,640]{2,1,0:T(8,128)(2,1)S(1)} %bitcast.6), custom_call_target="tpu_custom_call" | custom-call | tf_op jit(solution)/shard_map/pallas_call | solution.py:264
  28.2 0.6 %copy.9 = bf16[1,2,2688]{2,1,0:T(2,128)(2,1)} copy(bf16[1,2,2688]{2,1,0:T(2,128)(2,1)S(1)} %bitcast.9) | data formatting | bytes 21504
  28.8 0.6 %copy.10 = bf16[1,21,2,1280]{3,2,1,0:T(2,128)(2,1)} copy(bf16[1,21,2,1280]{3,2,1,0:T(2,128)(2,1)S(1)} %bitcast.8) | data formatting | bytes 215040
Async XLA Ops:
  0.6 0.7 %copy-start.2 = (s32[2,336]{1,0:T(2,128)S(1)}, s32[2,336]{1,0:T(2,128)}, u32[]{:S(2)}) copy-start(s32[2,336]{1,0:T(2,128)} %wave_ref.1) | copy-start | bytes 8068
  0.6 0.7 %copy-start.3 = (s32[2]{0:T(128)S(1)}, s32[2]{0:T(128)}, u32[]{:S(2)}) copy-start(s32[2]{0:T(128)} %length_ref.1) | copy-start | bytes 28
  1.3 1.2 %copy-start = (bf16[1,21,640,32]{2,3,1,0:T(8,128)(2,1)S(1)}, bf16[1,21,640,32]{2,3,1,0:T(8,128)(2,1)}, u32[]{:S(2)}) copy-start(bf16[1,21,640,32]{2,3,1,0:T(8,128)(2,1)} %param.6) | copy-start | bytes 2580484
  2.5 0.9 %copy-start.1 = (bf16[1,21,2,1280]{3,2,1,0:T(2,128)(2,1)S(1)}, bf16[1,21,2,1280]{3,2,1,0:T(2,128)(2,1)}, u32[]{:S(2)}) copy-start(bf16[1,21,2,1280]{3,2,1,0:T(2,128)(2,1)} %param.5) | copy-start | bytes 322564
  3.4 0.7 %copy-start.4 = (f32[32]{0:T(128)S(1)}, f32[32]{0:T(128)}, u32[]{:S(2)}) copy-start(f32[32]{0:T(128)} %quad_ref.1) | copy-start | bytes 388

commit v2 on v1

--- a/solution.py
+++ b/solution.py
@@ -11,8 +11,8 @@
 NLON = 2688
 LOW = 32
 HIGH = 24
-STEP = 384
-GROUP = 8
+STEP = 896
+GROUP = 32
 F32 = jnp.float32
 BF16 = jnp.bfloat16
 
@@ -51,8 +51,8 @@
 
 
 def kernel(
-    n_lat, n_lev, wave_ref, length_ref, quad_ref, spec_ref, leg_ref, grid_ref, out_ref,
-    four, stacked, send1, recv1, send2, recv2, columns, flipped, table_p, table_q, table_b, sems,
+    n_lat, n_lev, wave_in, length_in, quad_in, spec_in, leg_in, grid_ref, out_ref,
+    wave_ref, length_ref, quad_ref, spec_ref, leg_ref, load_sems, four, stacked, send1, recv1, send2, recv2, columns, flipped, table_p, table_q, table_b, sems,
 ):
     n = n_lat * n_lev
     lat = lax.axis_index("lat")
@@ -67,6 +67,13 @@
         other = lax.rem(me + t, n)
         return other, (lax.rem(other, n_lat), lax.div(other, n_lat))
 
+    pairs = (
+        (spec_in, spec_ref), (leg_in, leg_ref), (wave_in, wave_ref), (length_in, length_ref), (quad_in, quad_ref),
+    )
+    loads = [pltpu.make_async_copy(src, dst, load_sems.at[i]) for i, (src, dst) in enumerate(pairs)]
+    for load in loads:
+        load.start()
+
     barrier = pltpu.get_barrier_semaphore()
 
     def greet(t, carry):
@@ -79,6 +86,8 @@
     lane = lax.broadcasted_iota(jnp.int32, (1, 128), 1)
     wave_row = jnp.full((1, 128), float(M), F32)
     four[...] = jnp.zeros_like(four)
+    for load in loads:
+        load.wait()
     for s in range(own):
         m = wave_ref[lev, lat * own + s]
         x = spec_ref[s].astype(F32)
@@ -113,8 +122,7 @@
     for r in range(local):
         length = jnp.full((1, STEP), length_ref[r].astype(F32), F32)
 
-        def tables(i, carry):
-            at = pl.multiple_of(i * STEP, 128)
+        for at in range(0, NLON, STEP):
             k = (lax.broadcasted_iota(jnp.int32, (1, STEP), 1) + at).astype(F32)
             a = lax.broadcasted_iota(jnp.int32, (HIGH, STEP), 0).astype(F32) * float(LOW)
             cos_a, sin_a = turn_cos_sin(a * k, length)
@@ -125,9 +133,6 @@
             b = lax.broadcasted_iota(jnp.int32, (LOW, STEP), 0).astype(F32)
             cos_b, sin_b = turn_cos_sin(b * k, length)
             table_b[r, :, pl.ds(at, STEP)] = jnp.concatenate([cos_b, sin_b], 0)
-            return carry
-
-        lax.fori_loop(0, NLON // STEP, tables, 0)
 
     def all_arrived(buffer, k):
         part = buffer.at[pl.ds(0, n - 1)]
@@ -162,9 +167,8 @@
             totals[r] + dot_nt(left, jnp.concatenate(rights[r], 1).astype(BF16)) for r in range(local)
         )
 
-    placed = lax.fori_loop(
-        0, n // GROUP, place, tuple(jnp.zeros((LOW, 2 * HIGH), F32) for _ in range(local))
-    )
+    placed = tuple(jnp.zeros((LOW, 2 * HIGH), F32) for _ in range(local))
+    placed = place(0, placed) if n == GROUP else lax.fori_loop(0, n // GROUP, place, placed)
 
     row_b = lax.broadcasted_iota(jnp.int32, (LOW, 2 * HIGH), 0)
     col_a = lax.rem(lax.broadcasted_iota(jnp.int32, (LOW, 2 * HIGH), 1), HIGH)
@@ -175,8 +179,8 @@
         z = jnp.concatenate([z, z], 1).astype(BF16)
         length_int = length_ref[r]
 
-        def longitudes(i, total):
-            at = pl.multiple_of(i * STEP, 128)
+        total = jnp.zeros((4 * HIGH, 4 * LOW), F32)
+        for at in range(0, NLON, STEP):
             here = pl.ds(at, STEP)
             cos_b = table_b[r, pl.ds(0, LOW), here]
             sin_b = table_b[r, pl.ds(LOW, LOW), here]
@@ -189,11 +193,7 @@
             shaped = jnp.where(k < length_int, shaped, 0.0)
             columns[pl.ds(r, 1), here] = shaped
             g = jnp.concatenate([shaped * cos_b, shaped * sin_b], 0)
-            return total + dot_nt(q, jnp.concatenate(split(g), 0))
-
-        total = lax.fori_loop(
-            0, NLON // STEP, longitudes, jnp.zeros((4 * HIGH, 4 * LOW), F32)
-        )
+            total = total + dot_nt(q, jnp.concatenate(split(g), 0))
         both = 2 * HIGH
         total = total[:both, : 2 * LOW] + total[both:, : 2 * LOW] + total[:both, 2 * LOW :]
         ss, sc = total[:HIGH, LOW:], total[:HIGH, :LOW]
@@ -224,7 +224,10 @@
             send2[g * GROUP + i] = jnp.concatenate(lines, 0)
         return carry
 
-    lax.fori_loop(0, n // GROUP, pick, 0)
+    if n == GROUP:
+        pick(0, 0)
+    else:
+        lax.fori_loop(0, n // GROUP, pick, 0)
 
     def send_slots(t, carry):
         other, device = partner(t)
@@ -260,16 +263,22 @@
     rows_up = -(-rows // 128) * 128
     message = 4 if local < 4 else -(-(local + 1) // 8) * 8
     vmem = pl.BlockSpec(memory_space=pltpu.VMEM)
-    smem = pl.BlockSpec(memory_space=pltpu.SMEM)
+    anywhere = pl.BlockSpec(memory_space=pl.ANY)
     grid, out = pl.pallas_call(
         functools.partial(kernel, n_lat, n_lev),
         out_shape=(
             jax.ShapeDtypeStruct((local, NLON), BF16),
             jax.ShapeDtypeStruct((own, fields, double), BF16),
         ),
-        in_specs=[smem, smem, smem, vmem, vmem],
+        in_specs=[anywhere] * 5,
         out_specs=(vmem, vmem),
         scratch_shapes=[
+            pltpu.SMEM(slot_wave.shape, jnp.int32),
+            pltpu.SMEM(row_length.shape, jnp.int32),
+            pltpu.SMEM(quad_weight.shape, F32),
+            pltpu.VMEM((own, fields, double), BF16),
+            pltpu.VMEM((own, rows, deg), BF16),
+            pltpu.SemaphoreType.DMA((5,)),
             pltpu.VMEM((128, rows_up), F32),
             pltpu.VMEM((rows, 128), F32),
             pltpu.VMEM((n_lat, message, 128), F32),
@@ -284,7 +293,7 @@
             pltpu.SemaphoreType.DMA((4,)),
         ],
         compiler_params=pltpu.CompilerParams(
-            collective_id=0, has_side_effects=True, vmem_limit_bytes=48 * 1024 * 1024
+            collective_id=0, has_side_effects=True, vmem_limit_bytes=60 * 1024 * 1024
         ),
     )(
         slot_wave, row_length, quad_weight, spectral_in.reshape(own, fields, double),

time: 29.7 us -> 23.6 us (0.79)
  Pallas kernels: 24.2 us -> 19.8 us
  local copies, waits for them, and re-layouts: 4.63 us -> 2.92 us
    pallas_call x1, Pallas kernels: 24.2 us -> 19.8 us  [shards(): pl.pallas_call(functools.partial(kernel, n_lat, n_lev), out_shape=(jax.Sh...]
    unnamed x12 -> x2, local copies, waits for them, and re-layouts: 4.63 us -> 2.92 us
where the time goes in v2:
time: 23.6 us; the launch traced here: 23.4 us
  Pallas kernels  19.8 us (84%)
  local copies, waits for them, and re-layouts  2.92 us (12%)
  between operations  0.64 us (3%)
    pallas_call x1, Pallas kernels, shards(): pl.pallas_call(functools.partial(kernel, n_lat, n_lev), out_shape=(jax.Sh...  19.8 us
    unnamed x2, local copies, waits for them, and re-layouts  2.92 us

profile of v2, /device:TPU:0, one launch (start us, length us, event | category | flops | bytes accessed | tf_op | source)
XLA Modules:
  0.0 23.4 jit_solution(17740368634609911147)
XLA Ops:
  0.6 19.8 %shard_map.68 = (bf16[2,2688]{1,0:T(2,128)(2,1)}, bf16[21,2,1280]{2,1,0:T(2,128)(2,1)}) custom-call(s32[2,336]{1,0:T(2,128)} %wave_in.1, s32[2]{0:T(128)} %length_in.1, f32[32]{0:T(128)} %quad_in.1, bf16[21,2,1280]{2,1,0:T(2,128)(2,1)} %bitcast.7, bf16[21,32,640]{2,1,0:T(8,128)(2,1)} %bitcast.6), custom_call_target="tpu_custom_call" | custom-call | tf_op jit(solution)/shard_map/pallas_call | solution.py:267
  20.4 1.3 %copy.9 = bf16[1,2,2688]{2,1,0:T(2,128)(2,1)} copy(bf16[1,2,2688]{2,1,0:T(2,128)(2,1)} %bitcast.9) | data formatting | bytes 21504
  21.7 1.6 %copy.10 = bf16[1,21,2,1280]{3,2,1,0:T(2,128)(2,1)} copy(bf16[1,21,2,1280]{3,2,1,0:T(2,128)(2,1)} %bitcast.8) | data formatting | bytes 215040

commit v3 on v2

--- a/solution.py
+++ b/solution.py
@@ -52,7 +52,7 @@
 
 def kernel(
     n_lat, n_lev, wave_in, length_in, quad_in, spec_in, leg_in, grid_ref, out_ref,
-    wave_ref, length_ref, quad_ref, spec_ref, leg_ref, load_sems, four, stacked, send1, recv1, send2, recv2, columns, flipped, table_p, table_q, table_b, sems,
+    wave_ref, length_ref, quad_ref, spec_ref, leg_ref, load_sems, four, stacked, send1, recv1, send2, recv2, columns, flipped, table_a, table_b, sems,
 ):
     n = n_lat * n_lev
     lat = lax.axis_index("lat")
@@ -82,11 +82,29 @@
 
     lax.fori_loop(1, n, greet, 0)
 
+    loads[3].wait()
+    low = lax.broadcasted_iota(jnp.int32, (HIGH + LOW, 128), 0)
+    wave = jnp.where(low < HIGH, low * LOW, low - HIGH).astype(F32)
+    k = lax.broadcasted_iota(jnp.int32, (HIGH + LOW, 128), 1).astype(F32)
+    for r in range(local):
+        length = jnp.full((HIGH + LOW, 128), length_ref[r].astype(F32), F32)
+        cos_m, sin_m = turn_cos_sin(wave * k, length)
+        step_cos, step_sin = turn_cos_sin(wave * 128.0, length)
+        for at in range(0, NLON, 128):
+            here = pl.ds(at, 128)
+            a = jnp.concatenate([cos_m[:HIGH], sin_m[:HIGH]], 0)
+            table_a[r, :, here] = jnp.concatenate(split(a), 0)
+            table_b[r, :, here] = jnp.concatenate([cos_m[HIGH:], -sin_m[HIGH:]], 0)
+            cos_m, sin_m = (
+                cos_m * step_cos - sin_m * step_sin,
+                sin_m * step_cos + cos_m * step_sin,
+            )
+
     degree = lax.broadcasted_iota(jnp.int32, (per_slot, deg), 1)
     lane = lax.broadcasted_iota(jnp.int32, (1, 128), 1)
     wave_row = jnp.full((1, 128), float(M), F32)
     four[...] = jnp.zeros_like(four)
-    for load in loads:
+    for load in loads[:3] + loads[4:]:
         load.wait()
     for s in range(own):
         m = wave_ref[lev, lat * own + s]
@@ -119,21 +137,6 @@
     lax.fori_loop(1, n, send_rows, 0)
     recv1[me] = send1[lat]
 
-    for r in range(local):
-        length = jnp.full((1, STEP), length_ref[r].astype(F32), F32)
-
-        for at in range(0, NLON, STEP):
-            k = (lax.broadcasted_iota(jnp.int32, (1, STEP), 1) + at).astype(F32)
-            a = lax.broadcasted_iota(jnp.int32, (HIGH, STEP), 0).astype(F32) * float(LOW)
-            cos_a, sin_a = turn_cos_sin(a * k, length)
-            p = jnp.concatenate([cos_a, -sin_a], 0)
-            q = jnp.concatenate([sin_a, cos_a], 0)
-            table_p[r, :, pl.ds(at, STEP)] = jnp.concatenate(split(p), 0)
-            table_q[r, :, pl.ds(at, STEP)] = jnp.concatenate(split(q), 0)
-            b = lax.broadcasted_iota(jnp.int32, (LOW, STEP), 0).astype(F32)
-            cos_b, sin_b = turn_cos_sin(b * k, length)
-            table_b[r, :, pl.ds(at, STEP)] = jnp.concatenate([cos_b, sin_b], 0)
-
     def all_arrived(buffer, k):
         part = buffer.at[pl.ds(0, n - 1)]
         pltpu.make_async_copy(part, part, sems.at[k]).wait()
@@ -163,11 +166,10 @@
                 ]
                 rights[r].append(jnp.concatenate(pieces, 0))
         left = jnp.concatenate(lefts, 1).astype(BF16)
-        return tuple(
-            totals[r] + dot_nt(left, jnp.concatenate(rights[r], 1).astype(BF16)) for r in range(local)
-        )
-
-    placed = tuple(jnp.zeros((LOW, 2 * HIGH), F32) for _ in range(local))
+        right = jnp.concatenate([jnp.concatenate(side, 1) for side in rights], 0).astype(BF16)
+        return totals + dot_nt(left, right)
+
+    placed = jnp.zeros((LOW, 2 * HIGH * local), F32)
     placed = place(0, placed) if n == GROUP else lax.fori_loop(0, n // GROUP, place, placed)
 
     row_b = lax.broadcasted_iota(jnp.int32, (LOW, 2 * HIGH), 0)
@@ -175,32 +177,31 @@
     factor = jnp.where((row_b == 0) & (col_a == 0), 1.0, 2.0)
     spectra = []
     for r in range(local):
-        z = placed[r] * factor
-        z = jnp.concatenate([z, z], 1).astype(BF16)
+        z = placed[:, 2 * HIGH * r : 2 * HIGH * (r + 1)] * factor
+        z_re, z_im = z[:, :HIGH], z[:, HIGH:]
+        z = jnp.concatenate(
+            [jnp.concatenate([z_re, -z_im] * 2, 1), jnp.concatenate([z_im, z_re] * 2, 1)], 0
+        ).astype(BF16)
         length_int = length_ref[r]
 
         total = jnp.zeros((4 * HIGH, 4 * LOW), F32)
         for at in range(0, NLON, STEP):
             here = pl.ds(at, STEP)
-            cos_b = table_b[r, pl.ds(0, LOW), here]
-            sin_b = table_b[r, pl.ds(LOW, LOW), here]
-            q = table_q[r, :, here]
-            raw = jnp.sum(
-                dot_nn(z, table_p[r, :, here]) * cos_b - dot_nn(z, q) * sin_b, axis=0, keepdims=True
-            )
+            a = table_a[r, :, here]
+            b = table_b[r, :, here]
+            raw = jnp.sum(dot_nn(z, a) * b, axis=0, keepdims=True)
             shaped = (raw * (1.0 + 0.5 * jnp.tanh(raw))).astype(BF16).astype(F32)
             k = lax.broadcasted_iota(jnp.int32, (1, STEP), 1) + at
             shaped = jnp.where(k < length_int, shaped, 0.0)
             columns[pl.ds(r, 1), here] = shaped
-            g = jnp.concatenate([shaped * cos_b, shaped * sin_b], 0)
-            total = total + dot_nt(q, jnp.concatenate(split(g), 0))
+            total = total + dot_nt(a, jnp.concatenate(split(shaped * b), 0))
         both = 2 * HIGH
         total = total[:both, : 2 * LOW] + total[both:, : 2 * LOW] + total[:both, 2 * LOW :]
-        ss, sc = total[:HIGH, LOW:], total[:HIGH, :LOW]
-        cs, cc = total[HIGH:, LOW:], total[HIGH:, :LOW]
+        cc, cs = total[:HIGH, :LOW], total[:HIGH, LOW:]
+        sc, ss = total[HIGH:, :LOW], total[HIGH:, LOW:]
         length = jnp.full((HIGH, LOW), length_int.astype(F32), F32)
         weight = quad_ref[lat * local + r]
-        for part in (cc - ss, -(sc + cs)):
+        for part in (cc + ss, cs - sc):
             spectra.append((part / length).astype(BF16).astype(F32) * weight)
     grid_ref[...] = columns[pl.ds(0, local), :].astype(BF16)
     spectrum = jnp.concatenate(spectra, 0).astype(BF16)
@@ -263,14 +264,14 @@
     rows_up = -(-rows // 128) * 128
     message = 4 if local < 4 else -(-(local + 1) // 8) * 8
     vmem = pl.BlockSpec(memory_space=pltpu.VMEM)
-    anywhere = pl.BlockSpec(memory_space=pl.ANY)
+    hbm = pl.BlockSpec(memory_space=pltpu.HBM)
     grid, out = pl.pallas_call(
         functools.partial(kernel, n_lat, n_lev),
         out_shape=(
             jax.ShapeDtypeStruct((local, NLON), BF16),
             jax.ShapeDtypeStruct((own, fields, double), BF16),
         ),
-        in_specs=[anywhere] * 5,
+        in_specs=[hbm] * 5,
         out_specs=(vmem, vmem),
         scratch_shapes=[
             pltpu.SMEM(slot_wave.shape, jnp.int32),
@@ -288,12 +289,11 @@
             pltpu.VMEM((8, NLON), F32),
             pltpu.VMEM((128, rows), F32),
             pltpu.VMEM((local, 4 * HIGH, NLON), BF16),
-            pltpu.VMEM((local, 4 * HIGH, NLON), BF16),
             pltpu.VMEM((local, 2 * LOW, NLON), F32),
             pltpu.SemaphoreType.DMA((4,)),
         ],
         compiler_params=pltpu.CompilerParams(
-            collective_id=0, has_side_effects=True, vmem_limit_bytes=60 * 1024 * 1024
+            collective_id=0, has_side_effects=True, vmem_limit_bytes=55000 * 1024
         ),
     )(
         slot_wave, row_length, quad_weight, spectral_in.reshape(own, fields, double),

time: 23.6 us -> 22.8 us (0.966)
  Pallas kernels: 19.8 us -> 19.3 us
  local copies, waits for them, and re-layouts: 2.92 us -> 2.57 us
    pallas_call x1, Pallas kernels: 19.8 us -> 19.3 us  [shards(): pl.pallas_call(functools.partial(kernel, n_lat, n_lev), out_shape=(jax.Sh...]
    unnamed x2 -> x8, local copies, waits for them, and re-layouts: 2.92 us -> 2.57 us
where the time goes in v3:
time: 22.8 us; the launch traced here: 22.6 us
  Pallas kernels  19.3 us (85%)
  local copies, waits for them, and re-layouts  2.57 us (11%)
  between operations  0.66 us (3%)
    pallas_call x1, Pallas kernels, shards(): pl.pallas_call(functools.partial(kernel, n_lat, n_lev), out_shape=(jax.Sh...  19.3 us
    unnamed x8, local copies, waits for them, and re-layouts  2.57 us

profile of v3, /device:TPU:0, one launch (start us, length us, event | category | flops | bytes accessed | tf_op | source)
XLA Modules:
  0.0 22.6 jit_solution(7747466849239962401)
XLA Ops:
  0.6 0.0 copy-start
  0.6 0.0 copy-start.1
  0.7 0.7 %copy-done = s32[2,336]{1,0:T(2,128)S(1)} copy-done((s32[2,336]{1,0:T(2,128)S(1)}, s32[2,336]{1,0:T(2,128)}, u32[]{:S(2)}) %copy-start) | copy-done | bytes 2712
  1.3 0.0 copy-done.1
  1.3 0.0 copy-start.2
  1.3 0.7 %copy-done.2 = f32[32]{0:T(128)S(1)} copy-done((f32[32]{0:T(128)S(1)}, f32[32]{0:T(128)}, u32[]{:S(2)}) %copy-start.2) | copy-done | bytes 152
  2.0 19.3 %shard_map.68 = (bf16[2,2688]{1,0:T(2,128)(2,1)S(1)}, bf16[21,2,1280]{2,1,0:T(2,128)(2,1)S(1)}) custom-call(s32[2,336]{1,0:T(2,128)S(1)} %copy-done, s32[2]{0:T(128)S(1)} %copy-done.1, f32[32]{0:T(128)S(1)} %copy-done.2, bf16[21,2,1280]{2,1,0:T(2,128)(2,1)} %bitcast.9, bf16[21,32,640]{2,1,0:T(8,128)(2,1)} %bitcast.8), custom_call_target="tpu_custom_call" | custom-call | tf_op jit(solution)/shard_map/pallas_call | solution.py:268
  21.3 0.6 %copy.9 = bf16[1,2,2688]{2,1,0:T(2,128)(2,1)} copy(bf16[1,2,2688]{2,1,0:T(2,128)(2,1)S(1)} %bitcast.7) | data formatting | bytes 21504
  21.9 0.6 %copy.10 = bf16[1,21,2,1280]{3,2,1,0:T(2,128)(2,1)} copy(bf16[1,21,2,1280]{3,2,1,0:T(2,128)(2,1)S(1)} %bitcast.6) | data formatting | bytes 215040
Async XLA Ops:
  0.6 0.7 %copy-start = (s32[2,336]{1,0:T(2,128)S(1)}, s32[2,336]{1,0:T(2,128)}, u32[]{:S(2)}) copy-start(s32[2,336]{1,0:T(2,128)} %wave_in.1) | copy-start | bytes 8068
  0.6 0.7 %copy-start.1 = (s32[2]{0:T(128)S(1)}, s32[2]{0:T(128)}, u32[]{:S(2)}) copy-start(s32[2]{0:T(128)} %length_in.1) | copy-start | bytes 28
  1.3 0.7 %copy-start.2 = (f32[32]{0:T(128)S(1)}, f32[32]{0:T(128)}, u32[]{:S(2)}) copy-start(f32[32]{0:T(128)} %quad_in.1) | copy-start | bytes 388

commit v4 on v3

--- a/solution.py
+++ b/solution.py
@@ -64,8 +64,27 @@
     per_slot = 2 * fields
 
     def partner(t):
-        other = lax.rem(me + t, n)
-        return other, (lax.rem(other, n_lat), lax.div(other, n_lat))
+        if isinstance(t, int):
+            j = lax.rem(lat + t // n_lev, n_lat) if t >= n_lev else lat
+            g = lax.rem(lev + t % n_lev, n_lev) if t % n_lev else lev
+        else:
+            j, g = lax.rem(lat + t // n_lev, n_lat), lax.rem(lev + t % n_lev, n_lev)
+        return g * n_lat + j, (j, g)
+
+    whole = n == GROUP
+    partners = [partner(t) for t in range(GROUP)] if whole else None
+
+    def each_partner(act):
+        if whole:
+            for t in range(1, n):
+                act(t, *partners[t])
+        else:
+
+            def body(t, carry):
+                act(t, *partner(t))
+                return carry
+
+            lax.fori_loop(1, n, body, 0)
 
     pairs = (
         (spec_in, spec_ref), (leg_in, leg_ref), (wave_in, wave_ref), (length_in, length_ref), (quad_in, quad_ref),
@@ -76,11 +95,10 @@
 
     barrier = pltpu.get_barrier_semaphore()
 
-    def greet(t, carry):
-        pl.semaphore_signal(barrier, inc=1, device_id=partner(t)[1], device_id_type=pl.DeviceIdType.MESH)
-        return carry
-
-    lax.fori_loop(1, n, greet, 0)
+    def greet(t, other, device):
+        pl.semaphore_signal(barrier, inc=1, device_id=device, device_id_type=pl.DeviceIdType.MESH)
+
+    each_partner(greet)
 
     loads[3].wait()
     low = lax.broadcasted_iota(jnp.int32, (HIGH + LOW, 128), 0)
@@ -129,12 +147,10 @@
             device_id=device, device_id_type=pl.DeviceIdType.MESH,
         )
 
-    def send_rows(t, carry):
-        _, device = partner(t)
+    def send_rows(t, other, device):
         remote(send1.at[device[0]], recv1.at[me], 0, device).start()
-        return carry
-
-    lax.fori_loop(1, n, send_rows, 0)
+
+    each_partner(send_rows)
     recv1[me] = send1[lat]
 
     def all_arrived(buffer, k):
@@ -156,7 +172,7 @@
         lefts = []
         rights = [[] for _ in range(local)]
         for i in range(GROUP):
-            o = g * GROUP + i
+            o = partners[i][0] if whole else g * GROUP + i
             hot_a, hot_b = one_hots(o)
             lefts.append(hot_b)
             for r in range(local):
@@ -170,7 +186,7 @@
         return totals + dot_nt(left, right)
 
     placed = jnp.zeros((LOW, 2 * HIGH * local), F32)
-    placed = place(0, placed) if n == GROUP else lax.fori_loop(0, n // GROUP, place, placed)
+    placed = place(0, placed) if whole else lax.fori_loop(0, n // GROUP, place, placed)
 
     row_b = lax.broadcasted_iota(jnp.int32, (LOW, 2 * HIGH), 0)
     col_a = lax.rem(lax.broadcasted_iota(jnp.int32, (LOW, 2 * HIGH), 1), HIGH)
@@ -207,7 +223,8 @@
     spectrum = jnp.concatenate(spectra, 0).astype(BF16)
 
     def pick(g, carry):
-        hots = [one_hots(g * GROUP + i) for i in range(GROUP)]
+        owners = [partners[i][0] if whole else g * GROUP + i for i in range(GROUP)]
+        hots = [one_hots(o) for o in owners]
         right = jnp.concatenate([hot_b for _, hot_b in hots], 1).astype(BF16)
         spread = dot_nn(spectrum, right)
         for i in range(GROUP):
@@ -222,21 +239,26 @@
                     )
                     line = jnp.where(which, value, line)
                 lines.append(line)
-            send2[g * GROUP + i] = jnp.concatenate(lines, 0)
+            lines = jnp.concatenate(lines, 0)
+            if not whole:
+                send2[owners[i]] = lines
+            elif i == 0:
+                recv2[me] = lines
+            else:
+                send2[i] = lines
+                remote(send2.at[i], recv2.at[me], 1, partners[i][1]).start()
         return carry
 
-    if n == GROUP:
+    if whole:
         pick(0, 0)
     else:
         lax.fori_loop(0, n // GROUP, pick, 0)
 
-    def send_slots(t, carry):
-        other, device = partner(t)
-        remote(send2.at[other], recv2.at[me], 1, device).start()
-        return carry
-
-    lax.fori_loop(1, n, send_slots, 0)
-    recv2[me] = send2[me]
+        def send_slots(t, other, device):
+            remote(send2.at[other], recv2.at[me], 1, device).start()
+
+        each_partner(send_slots)
+        recv2[me] = send2[me]
     all_arrived(recv2, 3)
 
     for j in range(n_lat):

time: 22.8 us -> 22.5 us (0.987)
    pallas_call x1, Pallas kernels: 19.3 us -> 19.1 us  [shards(): pl.pallas_call(functools.partial(kernel, n_lat, n_lev), out_shape=(jax.Sh...]
where the time goes in v4:
time: 22.5 us; the launch traced here: 22.3 us
  Pallas kernels  19.1 us (85%)
  local copies, waits for them, and re-layouts  2.57 us (11%)
  between operations  0.66 us (3%)
    pallas_call x1, Pallas kernels, shards(): pl.pallas_call(functools.partial(kernel, n_lat, n_lev), out_shape=(jax.Sh...  19.1 us
    unnamed x8, local copies, waits for them, and re-layouts  2.57 us

profile of v4, /device:TPU:0, one launch (start us, length us, event | category | flops | bytes accessed | tf_op | source)
XLA Modules:
  0.0 22.3 jit_solution(15278734026133356021)
XLA Ops:
  0.6 0.0 copy-start
  0.6 0.0 copy-start.1
  0.7 0.7 %copy-done = s32[2,336]{1,0:T(2,128)S(1)} copy-done((s32[2,336]{1,0:T(2,128)S(1)}, s32[2,336]{1,0:T(2,128)}, u32[]{:S(2)}) %copy-start) | copy-done | bytes 2712
  1.3 0.0 copy-done.1
  1.3 0.0 copy-start.2
  1.3 0.7 %copy-done.2 = f32[32]{0:T(128)S(1)} copy-done((f32[32]{0:T(128)S(1)}, f32[32]{0:T(128)}, u32[]{:S(2)}) %copy-start.2) | copy-done | bytes 152
  2.0 19.1 %shard_map.68 = (bf16[2,2688]{1,0:T(2,128)(2,1)S(1)}, bf16[21,2,1280]{2,1,0:T(2,128)(2,1)S(1)}) custom-call(s32[2,336]{1,0:T(2,128)S(1)} %copy-done, s32[2]{0:T(128)S(1)} %copy-done.1, f32[32]{0:T(128)S(1)} %copy-done.2, bf16[21,2,1280]{2,1,0:T(2,128)(2,1)} %bitcast.9, bf16[21,32,640]{2,1,0:T(8,128)(2,1)} %bitcast.8), custom_call_target="tpu_custom_call" | custom-call | tf_op jit(solution)/shard_map/pallas_call | solution.py:290
  21.1 0.6 %copy.9 = bf16[1,2,2688]{2,1,0:T(2,128)(2,1)} copy(bf16[1,2,2688]{2,1,0:T(2,128)(2,1)S(1)} %bitcast.7) | data formatting | bytes 21504
  21.7 0.6 %copy.10 = bf16[1,21,2,1280]{3,2,1,0:T(2,128)(2,1)} copy(bf16[1,21,2,1280]{3,2,1,0:T(2,128)(2,1)S(1)} %bitcast.6) | data formatting | bytes 215040
Async XLA Ops:
  0.6 0.7 %copy-start = (s32[2,336]{1,0:T(2,128)S(1)}, s32[2,336]{1,0:T(2,128)}, u32[]{:S(2)}) copy-start(s32[2,336]{1,0:T(2,128)} %wave_in.1) | copy-start | bytes 8068
  0.6 0.7 %copy-start.1 = (s32[2]{0:T(128)S(1)}, s32[2]{0:T(128)}, u32[]{:S(2)}) copy-start(s32[2]{0:T(128)} %length_in.1) | copy-start | bytes 28
  1.3 0.7 %copy-start.2 = (f32[32]{0:T(128)S(1)}, f32[32]{0:T(128)}, u32[]{:S(2)}) copy-start(f32[32]{0:T(128)} %quad_in.1) | copy-start | bytes 388

commit v5 on v4

--- a/solution.py
+++ b/solution.py
@@ -315,12 +315,15 @@
             pltpu.SemaphoreType.DMA((4,)),
         ],
         compiler_params=pltpu.CompilerParams(
-            collective_id=0, has_side_effects=True, vmem_limit_bytes=55000 * 1024
+            collective_id=0, has_side_effects=True, vmem_limit_bytes=48 * 1024 * 1024
         ),
-    )(
-        slot_wave, row_length, quad_weight, spectral_in.reshape(own, fields, double),
-        jnp.transpose(legendre.reshape(own, deg, rows), (0, 2, 1)),
-    )
+    )(*(
+        pltpu.with_memory_space_constraint(x, pltpu.HBM)
+        for x in (
+            slot_wave, row_length, quad_weight, spectral_in.reshape(own, fields, double),
+            jnp.transpose(legendre.reshape(own, deg, rows), (0, 2, 1)),
+        )
+    ))
     return grid[None], out[None]
 
 

time: 22.5 us -> 21.2 us (0.942)
  local copies, waits for them, and re-layouts: 2.57 us -> 1.24 us
    unnamed x8 -> x2, local copies, waits for them, and re-layouts: 2.57 us -> 1.24 us
where the time goes in v5:
time: 21.2 us; the launch traced here: 21.1 us
  Pallas kernels  19.2 us (91%)
  local copies, waits for them, and re-layouts  1.24 us (6%)
  between operations  0.64 us (3%)
    pallas_call x1, Pallas kernels, shards(): pl.pallas_call(functools.partial(kernel, n_lat, n_lev), out_shape=(jax.Sh...  19.2 us
    unnamed x2, local copies, waits for them, and re-layouts  1.24 us

profile of v5, /device:TPU:0, one launch (start us, length us, event | category | flops | bytes accessed | tf_op | source)
XLA Modules:
  0.0 21.1 jit_solution(1112445667527174965)
XLA Ops:
  0.6 19.2 %shard_map.68 = (bf16[2,2688]{1,0:T(2,128)(2,1)S(1)}, bf16[21,2,1280]{2,1,0:T(2,128)(2,1)S(1)}) custom-call(s32[2,336]{1,0:T(2,128)} %wave_in.1, s32[2]{0:T(128)} %length_in.1, f32[32]{0:T(128)} %quad_in.1, bf16[21,2,1280]{2,1,0:T(2,128)(2,1)} %bitcast.9, bf16[21,32,640]{2,1,0:T(8,128)(2,1)} %bitcast.8), custom_call_target="tpu_custom_call" | custom-call | tf_op jit(solution)/shard_map/pallas_call | solution.py:290
  19.8 0.6 %copy.9 = bf16[1,2,2688]{2,1,0:T(2,128)(2,1)} copy(bf16[1,2,2688]{2,1,0:T(2,128)(2,1)S(1)} %bitcast.7) | data formatting | bytes 21504
  20.4 0.6 %copy.10 = bf16[1,21,2,1280]{3,2,1,0:T(2,128)(2,1)} copy(bf16[1,21,2,1280]{3,2,1,0:T(2,128)(2,1)S(1)} %bitcast.6) | data formatting | bytes 215040

commit v6 on v5

--- a/solution.py
+++ b/solution.py
@@ -120,7 +120,6 @@
 
     degree = lax.broadcasted_iota(jnp.int32, (per_slot, deg), 1)
     lane = lax.broadcasted_iota(jnp.int32, (1, 128), 1)
-    wave_row = jnp.full((1, 128), float(M), F32)
     four[...] = jnp.zeros_like(four)
     for load in loads[:3] + loads[4:]:
         load.wait()
@@ -130,14 +129,9 @@
         x = jnp.concatenate([x[:, :deg], x[:, deg:]], 0)
         x = jnp.where(degree >= m, x, 0.0).astype(BF16)
         four[pl.ds(s * per_slot, per_slot), pl.ds(0, rows)] = dot_nt(x, leg_ref[s]).astype(BF16).astype(F32)
-        wave_row = jnp.where(lane // per_slot == s, m.astype(F32), wave_row)
     turned = four[...].T
     for j in range(n_lat):
-        send1[j, pl.ds(0, local), :] = turned[j * local : (j + 1) * local, :]
-        send1[j, pl.ds(local, 1), :] = wave_row
-        send1[j, pl.ds(local + 1, send1.shape[1] - local - 1), :] = jnp.zeros(
-            (send1.shape[1] - local - 1, 128), F32
-        )
+        send1[j] = turned[j * local : (j + 1) * local, :]
 
     pl.semaphore_wait(barrier, n - 1)
 
@@ -157,31 +151,43 @@
         part = buffer.at[pl.ds(0, n - 1)]
         pltpu.make_async_copy(part, part, sems.at[k]).wait()
 
-    all_arrived(recv1, 1)
-
     index_a = lax.broadcasted_iota(jnp.int32, (HIGH, 128), 0)
     index_b = lax.broadcasted_iota(jnp.int32, (LOW, 128), 0)
     is_real = lax.rem(lane, per_slot) == lev
     is_imag = lax.rem(lane, per_slot) == lev + fields
-
-    def one_hots(o):
-        w = recv1[o, pl.ds(local, 1), :].astype(jnp.int32)
-        return index_a == w // LOW, (index_b == w % LOW).astype(F32)
+    slot_of = lane // per_slot
+
+    def owners_of(g):
+        if whole:
+            return partners
+        numbers = [g * GROUP + i for i in range(GROUP)]
+        return [(o, (lax.rem(o, n_lat), lax.div(o, n_lat))) for o in numbers]
+
+    def one_hots(g):
+        highs, lows = [], []
+        for _, (j, level) in owners_of(g):
+            w = jnp.full((1, 128), M, jnp.int32)
+            for s in range(own):
+                w = jnp.where(slot_of == s, wave_ref[level, j * own + s], w)
+            highs.append(w // LOW)
+            lows.append((index_b == w % LOW).astype(F32))
+        return highs, jnp.concatenate(lows, 1).astype(BF16)
+
+    ready = one_hots(0) if whole else None
+
+    all_arrived(recv1, 1)
 
     def place(g, totals):
-        lefts = []
+        highs, left = ready if whole else one_hots(g)
         rights = [[] for _ in range(local)]
-        for i in range(GROUP):
-            o = partners[i][0] if whole else g * GROUP + i
-            hot_a, hot_b = one_hots(o)
-            lefts.append(hot_b)
+        for (o, _), high in zip(owners_of(g), highs):
+            hot_a = index_a == high
             for r in range(local):
                 z = recv1[o, pl.ds(r, 1), :]
                 pieces = [
                     jnp.where(hot_a, jnp.where(which, z, 0.0), 0.0) for which in (is_real, is_imag)
                 ]
                 rights[r].append(jnp.concatenate(pieces, 0))
-        left = jnp.concatenate(lefts, 1).astype(BF16)
         right = jnp.concatenate([jnp.concatenate(side, 1) for side in rights], 0).astype(BF16)
         return totals + dot_nt(left, right)
 
@@ -223,19 +229,19 @@
     spectrum = jnp.concatenate(spectra, 0).astype(BF16)
 
     def pick(g, carry):
-        owners = [partners[i][0] if whole else g * GROUP + i for i in range(GROUP)]
-        hots = [one_hots(o) for o in owners]
-        right = jnp.concatenate([hot_b for _, hot_b in hots], 1).astype(BF16)
+        owners = [o for o, _ in owners_of(g)]
+        highs, right = ready if whole else one_hots(g)
         spread = dot_nn(spectrum, right)
         for i in range(GROUP):
             cut = spread[:, i * 128 : (i + 1) * 128]
+            hot_a = index_a == highs[i]
             lines = []
             for r in range(local):
                 line = jnp.zeros((1, 128), F32)
                 for c, which in enumerate((is_real, is_imag)):
                     first = (2 * r + c) * HIGH
                     value = jnp.sum(
-                        jnp.where(hots[i][0], cut[first : first + HIGH], 0.0), axis=0, keepdims=True
+                        jnp.where(hot_a, cut[first : first + HIGH], 0.0), axis=0, keepdims=True
                     )
                     line = jnp.where(which, value, line)
                 lines.append(line)
@@ -284,7 +290,6 @@
     n = n_lat * n_lev
     assert fields == n_lev and own * fields * 2 <= 128 and n % GROUP == 0 and rows % 8 == 0
     rows_up = -(-rows // 128) * 128
-    message = 4 if local < 4 else -(-(local + 1) // 8) * 8
     vmem = pl.BlockSpec(memory_space=pltpu.VMEM)
     hbm = pl.BlockSpec(memory_space=pltpu.HBM)
     grid, out = pl.pallas_call(
@@ -304,8 +309,8 @@
             pltpu.SemaphoreType.DMA((5,)),
             pltpu.VMEM((128, rows_up), F32),
             pltpu.VMEM((rows, 128), F32),
-            pltpu.VMEM((n_lat, message, 128), F32),
-            pltpu.VMEM((n, message, 128), F32),
+            pltpu.VMEM((n_lat, local, 128), F32),
+            pltpu.VMEM((n, local, 128), F32),
             pltpu.VMEM((n, local, 128), F32),
             pltpu.VMEM((n, local, 128), F32),
             pltpu.VMEM((8, NLON), F32),

time: 21.2 us -> 21 us (level)
    pallas_call x1, Pallas kernels: 19.2 us -> 19 us  [shards(): pl.pallas_call(functools.partial(kernel, n_lat, n_lev), out_shape=(jax.Sh...]
where the time goes in v6:
time: 21 us; the launch traced here: 20.8 us
  Pallas kernels  19 us (90%)
  local copies, waits for them, and re-layouts  1.24 us (6%)
  between operations  0.64 us (3%)
    pallas_call x1, Pallas kernels, shards(): pl.pallas_call(functools.partial(kernel, n_lat, n_lev), out_shape=(jax.Sh...  19 us
    unnamed x2, local copies, waits for them, and re-layouts  1.24 us

profile of v6, /device:TPU:0, one launch (start us, length us, event | category | flops | bytes accessed | tf_op | source)
XLA Modules:
  0.0 20.8 jit_solution(13982251776196021567)
XLA Ops:
  0.6 19.0 %shard_map.68 = (bf16[2,2688]{1,0:T(2,128)(2,1)S(1)}, bf16[21,2,1280]{2,1,0:T(2,128)(2,1)S(1)}) custom-call(s32[2,336]{1,0:T(2,128)} %wave_in.1, s32[2]{0:T(128)} %length_in.1, f32[32]{0:T(128)} %quad_in.1, bf16[21,2,1280]{2,1,0:T(2,128)(2,1)} %bitcast.9, bf16[21,32,640]{2,1,0:T(8,128)(2,1)} %bitcast.8), custom_call_target="tpu_custom_call" | custom-call | tf_op jit(solution)/shard_map/pallas_call | solution.py:295
  19.6 0.6 %copy.9 = bf16[1,2,2688]{2,1,0:T(2,128)(2,1)} copy(bf16[1,2,2688]{2,1,0:T(2,128)(2,1)S(1)} %bitcast.7) | data formatting | bytes 21504
  20.2 0.6 %copy.10 = bf16[1,21,2,1280]{3,2,1,0:T(2,128)(2,1)} copy(bf16[1,21,2,1280]{3,2,1,0:T(2,128)(2,1)S(1)} %bitcast.6) | data formatting | bytes 215040

commit v7 on v6

--- a/solution.py
+++ b/solution.py
@@ -86,9 +86,10 @@
 
             lax.fori_loop(1, n, body, 0)
 
-    pairs = (
-        (spec_in, spec_ref), (leg_in, leg_ref), (wave_in, wave_ref), (length_in, length_ref), (quad_in, quad_ref),
-    )
+    part = own // 3 if own % 3 == 0 else own
+    pairs = [(length_in, length_ref), (wave_in, wave_ref), (spec_in, spec_ref)]
+    pairs += [(leg_in.at[pl.ds(i, part)], leg_ref.at[pl.ds(i, part)]) for i in range(0, own, part)]
+    pairs.append((quad_in, quad_ref))
     loads = [pltpu.make_async_copy(src, dst, load_sems.at[i]) for i, (src, dst) in enumerate(pairs)]
     for load in loads:
         load.start()
@@ -100,7 +101,7 @@
 
     each_partner(greet)
 
-    loads[3].wait()
+    loads[0].wait()
     low = lax.broadcasted_iota(jnp.int32, (HIGH + LOW, 128), 0)
     wave = jnp.where(low < HIGH, low * LOW, low - HIGH).astype(F32)
     k = lax.broadcasted_iota(jnp.int32, (HIGH + LOW, 128), 1).astype(F32)
@@ -121,9 +122,11 @@
     degree = lax.broadcasted_iota(jnp.int32, (per_slot, deg), 1)
     lane = lax.broadcasted_iota(jnp.int32, (1, 128), 1)
     four[...] = jnp.zeros_like(four)
-    for load in loads[:3] + loads[4:]:
-        load.wait()
+    loads[1].wait()
+    loads[2].wait()
     for s in range(own):
+        if s % part == 0:
+            loads[3 + s // part].wait()
         m = wave_ref[lev, lat * own + s]
         x = spec_ref[s].astype(F32)
         x = jnp.concatenate([x[:, :deg], x[:, deg:]], 0)
@@ -175,6 +178,7 @@
 
     ready = one_hots(0) if whole else None
 
+    loads[-1].wait()
     all_arrived(recv1, 1)
 
     def place(g, totals):
@@ -306,7 +310,7 @@
             pltpu.SMEM(quad_weight.shape, F32),
             pltpu.VMEM((own, fields, double), BF16),
             pltpu.VMEM((own, rows, deg), BF16),
-            pltpu.SemaphoreType.DMA((5,)),
+            pltpu.SemaphoreType.DMA((7,)),
             pltpu.VMEM((128, rows_up), F32),
             pltpu.VMEM((rows, 128), F32),
             pltpu.VMEM((n_lat, local, 128), F32),

time: 21 us -> 21 us (level)
  no operation moved by 1% of the time
where the time goes in v7:
time: 21 us; the launch traced here: 20.9 us
  Pallas kernels  19 us (90%)
  local copies, waits for them, and re-layouts  1.24 us (6%)
  between operations  0.64 us (3%)
    pallas_call x1, Pallas kernels, shards(): pl.pallas_call(functools.partial(kernel, n_lat, n_lev), out_shape=(jax.Sh...  19 us
    unnamed x2, local copies, waits for them, and re-layouts  1.24 us

profile of v7, /device:TPU:0, one launch (start us, length us, event | category | flops | bytes accessed | tf_op | source)
XLA Modules:
  0.0 20.9 jit_solution(16309182734423231567)
XLA Ops:
  0.6 19.0 %shard_map.68 = (bf16[2,2688]{1,0:T(2,128)(2,1)S(1)}, bf16[21,2,1280]{2,1,0:T(2,128)(2,1)S(1)}) custom-call(s32[2,336]{1,0:T(2,128)} %wave_in.1, s32[2]{0:T(128)} %length_in.1, f32[32]{0:T(128)} %quad_in.1, bf16[21,2,1280]{2,1,0:T(2,128)(2,1)} %bitcast.9, bf16[21,32,640]{2,1,0:T(8,128)(2,1)} %bitcast.8), custom_call_target="tpu_custom_call" | custom-call | tf_op jit(solution)/shard_map/pallas_call | solution.py:299
  19.6 0.6 %copy.9 = bf16[1,2,2688]{2,1,0:T(2,128)(2,1)} copy(bf16[1,2,2688]{2,1,0:T(2,128)(2,1)S(1)} %bitcast.7) | data formatting | bytes 21504
  20.2 0.6 %copy.10 = bf16[1,21,2,1280]{3,2,1,0:T(2,128)(2,1)} copy(bf16[1,21,2,1280]{3,2,1,0:T(2,128)(2,1)S(1)} %bitcast.6) | data formatting | bytes 215040
